TPU v7x, 32 devices: a whole 2x2x4 slice. The times are simulated.
32 devices in a mesh: groups: 2 (over y), node: 4 (over x, core), local: 4 (over z).
Axes of the slice: x: 2, y: 2, z: 4, core: 2. Of those that a mesh axis runs over, the one named last changes fastest.
Arguments:
- tokens_in: bfloat16 [2, 2048, 3584], P(None, ('groups', 'node', 'local')), parts along dimension 1, may hold values from -6 to 6
- expert_ids: int32 [2, 2048, 4], P(None, ('groups', 'node', 'local')), parts along dimension 1, may hold values from 0 to 7, as said below
- gate_fixed: int32 [2, 2048, 4], P(None, ('groups', 'node', 'local')), parts along dimension 1, may hold values from 1 to 65535
- w_gate: bfloat16 [16, 3584, 512], P(('node', 'local')), may hold values from -0.09375 to 0.09375
- w_up: bfloat16 [16, 3584, 512], P(('node', 'local')), may hold values from -0.09375 to 0.09375
- w_down: bfloat16 [16, 512, 3584], P(('node', 'local')), may hold values from -0.1875 to 0.1875
Outputs:
- mixed: bfloat16 [2, 2048, 3584], P(None, ('groups', 'node', 'local')), parts along dimension 1
There are 2 independent parts, one for each index of `groups`. A program takes and returns all parts, laid end to end along the dimension named above; an argument that names none is the same for every part. Nothing has to cross between parts.
Inputs may be any that keep to these rules, and one draw needn't show every extreme that they name: `expert_ids`: each token names 4 different experts. Among the 64 tokens of one device in one micro-batch (aligned blocks of 64 tokens) no expert is named by more than 40 tokens, and one expert, the same in every block of a draw, is named by exactly 40.
All inputs are finite; a program needn't handle non-finite values.
Results may differ from a plain program's by a relative error of at most 0.0066.
Values may be sent and summed in bfloat16 or wider, within the bound.
A program may use at most 128 MiB of HBM per device.

v0:
```python
import jax
import jax.numpy as jnp
from jax import lax
from jax.sharding import PartitionSpec as P

route_scale = 2.5


def expert_part(block, gate_half, up_half, down_half):
    block_shape = block.shape
    expert_rows = block.reshape(-1, block_shape[-1])
    gate_act = jnp.dot(expert_rows, gate_half, preferred_element_type=jnp.float32)
    up_act = jnp.dot(expert_rows, up_half, preferred_element_type=jnp.float32)
    hidden = (jax.nn.silu(gate_act) * up_act).astype(jnp.bfloat16)
    partial_out = jnp.dot(hidden, down_half, preferred_element_type=jnp.float32).astype(
        jnp.bfloat16
    )
    return partial_out.reshape(block_shape)


def shards(tokens_in, expert_ids, gate_fixed, w_gate, w_up, w_down):
    node_count = lax.axis_size("node")
    local_count = lax.axis_size("local")
    experts_node = local_count // 2
    experts = node_count * experts_node
    batches, tok_rows, width = tokens_in.shape
    top_count = expert_ids.shape[2]
    capacity = 5 * tok_rows * top_count // (4 * experts)
    gate_half = w_gate[0]
    up_half = w_up[0]
    down_half = w_down[0]
    results = []
    for micro_batch in range(batches):
        chosen = expert_ids[micro_batch]
        fixed_gate = gate_fixed[micro_batch].astype(jnp.float32)
        weight = route_scale * fixed_gate / jnp.sum(fixed_gate, axis=1, keepdims=True)
        onehot = (chosen[:, :, None] == jnp.arange(experts, dtype=jnp.int32)[None, None, :]).astype(
            jnp.int32
        )
        onehot = onehot.reshape(tok_rows * top_count, experts)
        before = jnp.cumsum(onehot, axis=0) - onehot
        slot_rank = jnp.sum(before * onehot, axis=1).reshape(tok_rows, top_count)
        position = chosen * capacity + slot_rank
        select = jnp.any(
            position[None, :, :] == jnp.arange(experts * capacity, dtype=jnp.int32)[:, None, None],
            axis=2,
        )
        packed = jnp.dot(
            select.astype(jnp.bfloat16), tokens_in[micro_batch], preferred_element_type=jnp.float32
        ).astype(jnp.bfloat16)
        blocks_grid = packed.reshape(node_count, experts_node, capacity, width)
        copies = jnp.repeat(blocks_grid, 2, axis=1).reshape(
            node_count * local_count, capacity, width
        )
        partial_value = expert_part(
            lax.all_to_all(copies, ("node", "local"), split_axis=0, concat_axis=0, tiled=True),
            gate_half,
            up_half,
            down_half,
        )
        partial_value = partial_value.reshape(node_count, local_count, capacity, width)
        returned = lax.all_to_all(
            partial_value.reshape(node_count * local_count, capacity, width),
            ("node", "local"),
            split_axis=0,
            concat_axis=0,
            tiled=True,
        )
        halves = returned.reshape(node_count, experts_node, 2, capacity, width).astype(jnp.float32)
        outputs = (halves[:, :, 0] + halves[:, :, 1]).astype(jnp.bfloat16)
        lookup = outputs.reshape(experts * capacity, width)
        picked = (
            lookup[position.reshape(-1)].reshape(tok_rows, top_count, width).astype(jnp.float32)
        )
        mixed = jnp.sum(weight[:, :, None] * picked, axis=1)
        results.append(mixed.astype(jnp.bfloat16))
    return jnp.stack(results)


def solution(mesh):
    return jax.shard_map(
        shards,
        mesh=mesh,
        in_specs=(
            P(None, ("groups", "node", "local"), None),
            P(None, ("groups", "node", "local"), None),
            P(None, ("groups", "node", "local"), None),
            P(("node", "local"), None, None),
            P(("node", "local"), None, None),
            P(("node", "local"), None, None),
        ),
        out_specs=P(None, ("groups", "node", "local"), None),
        check_vma=False,
    )
```

profile of v0, /device:TPU:0, one launch (start us, length us, event | category | flops | bytes accessed | tf_op | source)
XLA Modules:
  0.0 461.7 jit_solution(10685066380527321700)
XLA Ops:
  0.0 0.7 fusion.38
  0.7 0.1 copy.33
  0.8 0.1 eq.86
  0.9 0.1 eq.82
  1.0 0.6 reduce-window.14
  1.6 0.2 slice_reduce_fusion.1
  1.9 0.1 fusion.35
  2.0 0.1 reshape.205
  2.1 0.1 copy.25
  2.2 0.1 fusion.30
  2.3 1.8 convolution_convert_fusion.3
  4.1 2.4 broadcast_in_dim.4
  6.5 0.0 copy-start.1
  6.5 7.5 %all-to-all-start = ((bf16[16,40,3584]{2,1,0:T(8,128)(2,1)}), bf16[16,40,3584]{2,1,0:T(8,128)(2,1)}, u32[]{:S(2)}, u32[]{:S(2)}) async-start(bf16[16,40,3584]{2,1,0:T(8,128)(2,1)} %bitcast.107), calls=%async_computation | async-start | bytes 9175040 | tf_op jit(solution)/shard_map/all_to_all | solution.py:56
  14.1 0.1 copy.36
  14.2 0.1 eq.98
  14.3 0.1 eq.94
  14.4 0.6 reduce-window.16
  15.0 0.2 slice_reduce_fusion
  15.2 0.1 fusion.33
  15.3 0.1 reshape.209
  15.5 0.1 copy.30
  15.5 0.1 fusion.31
  15.7 0.0 copy-done.1
  15.7 0.8 convolution_convert_fusion.2
  16.5 100.4 %all-to-all-done = bf16[16,40,3584]{2,1,0:T(8,128)(2,1)} async-done(((bf16[16,40,3584]{2,1,0:T(8,128)(2,1)}), bf16[16,40,3584]{2,1,0:T(8,128)(2,1)}, u32[]{:S(2)}, u32[]{:S(2)}) %all-to-all-start) | async-done | bytes 4587552 | tf_op jit(solution)/shard_map/all_to_all | solution.py:56
  116.9 2.5 broadcast_in_dim.5
  119.5 4.6 all-to-all-start.2
  124.1 0.0 copy-start.3
  124.1 6.1 %fusion.12 = f32[640,512]{1,0:T(8,128)S(1)} fusion(bf16[640,3584]{1,0:T(8,128)(2,1)} %bitcast.7, bf16[1,3584,512]{2,1,0:T(8,128)(2,1)} %param.9), kind=kOutput, calls=%fused_computation.22 | convolution fusion | flops 2348810240 | bytes 9568256 | tf_op jit(solution)/shard_map/dot_general | solution.py:12
  130.2 0.0 copy-done.3
  130.2 0.0 copy-start.5
  130.2 5.1 %fusion.23 = bf16[640,512]{1,0:T(8,128)(2,1)S(1)} fusion(bf16[640,3584]{1,0:T(8,128)(2,1)} %bitcast.7, bf16[1,3584,512]{2,1,0:T(8,128)(2,1)S(1)} %copy-done.3, f32[640,512]{1,0:T(8,128)S(1)} %fusion.12), kind=kOutput, calls=%fused_computation.29 | convolution fusion | flops 2350776320 | bytes 10223616 | tf_op jit(solution)/shard_map/dot_general | solution.py:13
  135.3 0.0 copy-done.5
  135.3 4.7 %convolution_convert_fusion.1 = bf16[640,3584]{1,0:T(8,128)(2,1)} fusion(bf16[640,512]{1,0:T(8,128)(2,1)S(1)} %fusion.23, bf16[1,512,3584]{2,1,0:T(8,128)(2,1)S(1)} %copy-done.5), kind=kOutput, calls=%fused_computation.3 | convolution fusion | flops 2351104000 | bytes 8912896 | tf_op jit(solution)/shard_map/dot_general | solution.py:15
  140.0 86.9 %all-to-all-done.2 = bf16[16,40,3584]{2,1,0:T(8,128)(2,1)} async-done(((bf16[16,40,3584]{2,1,0:T(8,128)(2,1)}), bf16[16,40,3584]{2,1,0:T(8,128)(2,1)}, u32[]{:S(2)}, u32[]{:S(2)}) %all-to-all-start.2) | async-done | bytes 4587552 | tf_op jit(solution)/shard_map/all_to_all | solution.py:56
  226.9 4.6 all-to-all-start.1
  231.4 0.0 copy-start.4
  231.5 6.1 %fusion.10 = f32[640,512]{1,0:T(8,128)S(1)} fusion(bf16[640,3584]{1,0:T(8,128)(2,1)} %bitcast.25, bf16[1,3584,512]{2,1,0:T(8,128)(2,1)} %param.9), kind=kOutput, calls=%fused_computation.20 | convolution fusion | flops 2348810240 | bytes 9568256 | tf_op jit(solution)/shard_map/dot_general | solution.py:12
  237.5 0.0 copy-done.4
  237.6 0.0 copy-start.6
  237.6 5.1 %fusion.20 = bf16[640,512]{1,0:T(8,128)(2,1)S(1)} fusion(bf16[640,3584]{1,0:T(8,128)(2,1)} %bitcast.25, bf16[1,3584,512]{2,1,0:T(8,128)(2,1)S(1)} %copy-done.4, f32[640,512]{1,0:T(8,128)S(1)} %fusion.10), kind=kOutput, calls=%fused_computation.28 | convolution fusion | flops 2350776320 | bytes 10223616 | tf_op jit(solution)/shard_map/dot_general | solution.py:13
  242.7 0.0 copy-done.6
  242.7 4.6 convolution_convert_fusion
  247.3 87.0 %all-to-all-done.1 = bf16[16,40,3584]{2,1,0:T(8,128)(2,1)} async-done(((bf16[16,40,3584]{2,1,0:T(8,128)(2,1)}), bf16[16,40,3584]{2,1,0:T(8,128)(2,1)}, u32[]{:S(2)}, u32[]{:S(2)}) %all-to-all-start.1) | async-done | bytes 4587552 | tf_op jit(solution)/shard_map/all_to_all | solution.py:62
  334.2 4.9 %all-to-all-start.3 = ((bf16[16,40,3584]{2,1,0:T(8,128)(2,1)}), bf16[16,40,3584]{2,1,0:T(8,128)(2,1)}, u32[]{:S(2)}, u32[]{:S(2)}) async-start(bf16[16,40,3584]{2,1,0:T(8,128)(2,1)} %bitcast.111), calls=%async_computation.3 | async-start | bytes 9175040 | tf_op jit(solution)/shard_map/all_to_all | solution.py:62
  339.1 0.1 mul.92
  339.2 0.0 copy-done.2
  339.3 0.1 copy.23
  339.4 0.1 mul.101
  339.5 0.1 copy.28
  339.6 3.5 convert.4
  343.2 0.5 fusion.3
  343.7 3.0 gather_fusion
  346.7 4.5 reshape.213
  351.2 90.5 %all-to-all-done.3 = bf16[16,40,3584]{2,1,0:T(8,128)(2,1)} async-done(((bf16[16,40,3584]{2,1,0:T(8,128)(2,1)}), bf16[16,40,3584]{2,1,0:T(8,128)(2,1)}, u32[]{:S(2)}, u32[]{:S(2)}) %all-to-all-start.3) | async-done | bytes 4587552 | tf_op jit(solution)/shard_map/all_to_all | solution.py:62
  441.8 3.5 convert.5
  445.3 0.5 fusion.1
  445.9 3.0 gather_fusion.1
  448.8 4.5 reshape.215
  453.4 4.7 %multiply_reduce_fusion.1 = bf16[64,3584]{1,0:T(8,128)(2,1)S(1)} fusion(f32[64,4,3584]{2,1,0:T(4,128)} %reshape.213, f32[64,4]{1,0:T(8,128)S(1)} %copy.23), kind=kLoop, calls=%fused_computation.25 | loop fusion | flops 1605632 | bytes 4129792 | tf_op jit(solution)/shard_map/reduce_sum | solution.py:75
  458.1 0.0 copy-done
  458.1 2.5 multiply_reduce_fusion
  460.7 1.0 pad_maximum_fusion
  (16 shorter events, 0.2 us)
Async XLA Ops:
  6.5 9.1 %copy-start.1 = (bf16[2,64,3584]{2,1,0:T(8,128)(2,1)S(1)}, bf16[2,64,3584]{2,1,0:T(8,128)(2,1)}, u32[]{:S(2)}) copy-start(bf16[2,64,3584]{2,1,0:T(8,128)(2,1)} %param.6) | copy-start | bytes 2752516
  6.5 110.4 %all-to-all-start = ((bf16[16,40,3584]{2,1,0:T(8,128)(2,1)}), bf16[16,40,3584]{2,1,0:T(8,128)(2,1)}, u32[]{:S(2)}, u32[]{:S(2)}) async-start(bf16[16,40,3584]{2,1,0:T(8,128)(2,1)} %bitcast.107), calls=%async_computation | async-start | bytes 9175040 | tf_op jit(solution)/shard_map/all_to_all | solution.py:56
  119.5 107.4 %all-to-all-start.2 = ((bf16[16,40,3584]{2,1,0:T(8,128)(2,1)}), bf16[16,40,3584]{2,1,0:T(8,128)(2,1)}, u32[]{:S(2)}, u32[]{:S(2)}) async-start(bf16[16,40,3584]{2,1,0:T(8,128)(2,1)} %bitcast.108), calls=%async_computation.2 | async-start | bytes 9175040 | tf_op jit(solution)/shard_map/all_to_all | solution.py:56
  124.1 6.1 %copy-start.3 = (bf16[1,3584,512]{2,1,0:T(8,128)(2,1)S(1)}, bf16[1,3584,512]{2,1,0:T(8,128)(2,1)}, u32[]{:S(2)}) copy-start(bf16[1,3584,512]{2,1,0:T(8,128)(2,1)} %param.10) | copy-start | bytes 11010052
  130.2 5.1 %copy-start.5 = (bf16[1,512,3584]{2,1,0:T(8,128)(2,1)S(1)}, bf16[1,512,3584]{2,1,0:T(8,128)(2,1)}, u32[]{:S(2)}) copy-start(bf16[1,512,3584]{2,1,0:T(8,128)(2,1)} %param.11) | copy-start | bytes 11010052
  226.9 107.4 %all-to-all-start.1 = ((bf16[16,40,3584]{2,1,0:T(8,128)(2,1)}), bf16[16,40,3584]{2,1,0:T(8,128)(2,1)}, u32[]{:S(2)}, u32[]{:S(2)}) async-start(bf16[16,40,3584]{2,1,0:T(8,128)(2,1)} %bitcast.112), calls=%async_computation.1 | async-start | bytes 9175040 | tf_op jit(solution)/shard_map/all_to_all | solution.py:62
  231.4 6.1 %copy-start.4 = (bf16[1,3584,512]{2,1,0:T(8,128)(2,1)S(1)}, bf16[1,3584,512]{2,1,0:T(8,128)(2,1)}, u32[]{:S(2)}) copy-start(bf16[1,3584,512]{2,1,0:T(8,128)(2,1)} %param.10) | copy-start | bytes 11010052
  237.6 5.1 %copy-start.6 = (bf16[1,512,3584]{2,1,0:T(8,128)(2,1)S(1)}, bf16[1,512,3584]{2,1,0:T(8,128)(2,1)}, u32[]{:S(2)}) copy-start(bf16[1,512,3584]{2,1,0:T(8,128)(2,1)} %param.11) | copy-start | bytes 11010052
  334.2 5.0 %copy-start.2 = (s32[2,64,4]{1,2,0:T(4,128)S(1)}, s32[2,64,4]{1,2,0:T(4,128)}, u32[]{:S(2)}) copy-start(s32[2,64,4]{1,2,0:T(4,128)} %param.8) | copy-start | bytes 6148
  334.2 107.5 %all-to-all-start.3 = ((bf16[16,40,3584]{2,1,0:T(8,128)(2,1)}), bf16[16,40,3584]{2,1,0:T(8,128)(2,1)}, u32[]{:S(2)}, u32[]{:S(2)}) async-start(bf16[16,40,3584]{2,1,0:T(8,128)(2,1)} %bitcast.111), calls=%async_computation.3 | async-start | bytes 9175040 | tf_op jit(solution)/shard_map/all_to_all | solution.py:62
  453.4 4.7 %copy-start = (f32[64,4,3584]{2,1,0:T(4,128)S(1)}, f32[64,4,3584]{2,1,0:T(4,128)}, u32[]{:S(2)}) copy-start(f32[64,4,3584]{2,1,0:T(4,128)} %reshape.215) | copy-start | bytes 11010052
where the time goes:
time: 462 us
  waiting for transfers between devices  365 us (79%)
  matrix products  34.3 us (7%)
  local copies, waits for them, and re-layouts  22.5 us (5%)
  starting transfers between devices  21.5 us (5%)
  other arithmetic  18.2 us (4%)
    all_to_all x2, waiting for transfers between devices, shards(): lax.all_to_all(copies, ('node', 'local'), split_axis=0, concat_axis=0, ti...  187 us
    all_to_all x2, waiting for transfers between devices, shards(): lax.all_to_all(partial_value.reshape(node_count * local_count, capacity,...  177 us
    dot_general x2, matrix products, expert_part(): jnp.dot(expert_rows, gate_half, preferred_element_type=jnp.float32)  12.2 us
    all_to_all x2, starting transfers between devices, shards(): lax.all_to_all(copies, ('node', 'local'), split_axis=0, concat_axis=0, ti...  12.1 us
    dot_general x2, matrix products, expert_part(): up_act = jnp.dot(expert_rows, up_half, preferred_element_type=jnp.float32)  10.2 us
    all_to_all x2, starting transfers between devices, shards(): lax.all_to_all(partial_value.reshape(node_count * local_count, capacity,...  9.46 us
    dot_general x2, matrix products, expert_part(): jnp.dot(hidden, down_half, preferred_element_type=jnp.float32)  9.29 us
  transfers between devices with their start and end apart: 4, of which 4 were waited for; matrix products, arithmetic and copies ran while one was open for 10% of the time, Pallas kernels for 0%

commit v1 on v0

--- a/solution.py
+++ b/solution.py
@@ -1,7 +1,16 @@
+import functools
+
 import jax
 import jax.numpy as jnp
 from jax import lax
+from jax.experimental import pallas as pl
+from jax.experimental.pallas import tpu as pltpu
 from jax.sharding import PartitionSpec as P
+
+MESH = pl.DeviceIdType.MESH
+lines_z = 4
+rows_chunk = 256
+cols_tile = 256
 
 route_scale = 2.5
 
@@ -77,9 +86,368 @@
     return jnp.stack(results)
 
 
+z_steps = ((3, 1), (0, -1), (2, 1), (1, -1), (1, 1), (2, -1))
+
+
+def gather_kernel(
+    tokens, cols, gate_hbm, up_hbm, down_hbm, out,
+    g, p, core_in, x_in, z_in, gate_w, up_w, down_w, hidden,
+    load_sem, g_send, g_recv, c_send, c_recv, x_send, x_recv, z_send, z_recv,
+):
+    batches, tok, width = tokens.shape
+    half_units = gate_w.shape[1]
+    group = lax.axis_index("groups")
+    node = lax.axis_index("node")
+    z = lax.axis_index("local")
+    x, core = node // 2, node % 2
+    expert = node * (lines_z // 2) + z // 2
+    other_x, other_core = 1 - x, 1 - core
+    to_x = (group, other_x * 2 + core, z)
+    to_core = (group, x * 2 + other_core, z)
+    to_high = (group, node, z + 1)
+    to_low = (group, node, z - 1)
+
+    def slot(xs, zs, cs):
+        return (xs * lines_z + zs) * 2 + cs
+
+    def at_rows(index):
+        return pl.ds(pl.multiple_of(index * tok, tok), tok)
+
+    mine = slot(x, z, core)
+    loads = []
+    for batch in range(batches):
+        loads.append(
+            pltpu.make_async_copy(
+                tokens.at[batch], g.at[batch, at_rows(mine), pl.ds(0, width)], load_sem.at[batch]
+            )
+        )
+    loads.append(pltpu.make_async_copy(gate_hbm.at[0], gate_w, load_sem.at[2]))
+    loads.append(pltpu.make_async_copy(up_hbm.at[0], up_w, load_sem.at[3]))
+    loads.append(pltpu.make_async_copy(down_hbm.at[0], down_w, load_sem.at[4]))
+    for load in loads:
+        load.start()
+    for batch in range(batches):
+        g[batch, at_rows(mine), pl.ds(width, 128)] = cols[batch]
+
+    barrier = pltpu.get_barrier_semaphore()
+    pl.semaphore_signal(barrier, inc=1, device_id=to_x, device_id_type=MESH)
+    pl.semaphore_signal(barrier, inc=1, device_id=to_core, device_id_type=MESH)
+
+    @pl.when(z < lines_z - 1)
+    def _():
+        pl.semaphore_signal(barrier, inc=1, device_id=to_high, device_id_type=MESH)
+
+    @pl.when(z > 0)
+    def _():
+        pl.semaphore_signal(barrier, inc=1, device_id=to_low, device_id_type=MESH)
+
+    pl.semaphore_wait(barrier, 3 + (z + 1) % lines_z // 2)
+
+    def g_copy(batch, index, kind, target):
+        part = g.at[batch, at_rows(index)]
+        return pltpu.make_async_remote_copy(
+            src_ref=part, dst_ref=part,
+            send_sem=g_send.at[batch, kind, index], recv_sem=g_recv.at[batch, index],
+            device_id=target, device_id_type=MESH,
+        )
+
+    def arrived(batch, index):
+        g_copy(batch, index, 3, to_core).wait_recv()
+
+    def gather_own(batch):
+        loads[batch].wait()
+        g_copy(batch, mine, 2, to_x).start()
+
+        @pl.when(z < lines_z - 1)
+        def _():
+            g_copy(batch, mine, 0, to_high).start()
+
+        @pl.when(z > 0)
+        def _():
+            g_copy(batch, mine, 1, to_low).start()
+
+        g_copy(batch, mine, 3, to_core).start()
+
+    def gather_forward(batch, step):
+        @pl.when(z >= step)
+        def _():
+            index = slot(x, z - step, core)
+            arrived(batch, index)
+
+            @pl.when(z < lines_z - 1)
+            def _():
+                g_copy(batch, index, 0, to_high).start()
+
+            g_copy(batch, index, 2, to_x).start()
+            g_copy(batch, index, 3, to_core).start()
+
+        @pl.when(z + step < lines_z)
+        def _():
+            index = slot(x, z + step, core)
+            arrived(batch, index)
+
+            @pl.when(z > 0)
+            def _():
+                g_copy(batch, index, 1, to_low).start()
+
+            g_copy(batch, index, 2, to_x).start()
+            g_copy(batch, index, 3, to_core).start()
+
+    def gather_across(batch):
+        def one(zs):
+            index = slot(other_x, zs, core)
+            arrived(batch, index)
+            g_copy(batch, index, 3, to_core).start()
+
+        one(z)
+        for step in range(1, lines_z):
+            @pl.when(z >= step)
+            def _():
+                one(z - step)
+
+            @pl.when(z + step < lines_z)
+            def _():
+                one(z + step)
+
+    def gather_core(batch):
+        @pl.loop(0, 2 * lines_z)
+        def _(index):
+            arrived(batch, index * 2 + other_core)
+
+    def gather_sent(batch):
+        @pl.loop(0, lines_z)
+        def _(zs):
+            index = slot(x, zs, core)
+
+            @pl.when(jnp.logical_and(z < lines_z - 1, zs <= z))
+            def _():
+                g_copy(batch, index, 0, to_high).wait_send()
+
+            @pl.when(jnp.logical_and(z > 0, zs >= z))
+            def _():
+                g_copy(batch, index, 1, to_low).wait_send()
+
+            g_copy(batch, index, 2, to_x).wait_send()
+            g_copy(batch, index, 3, to_core).wait_send()
+            g_copy(batch, slot(other_x, zs, core), 3, to_core).wait_send()
+
+    def compute(batch, xs, pair):
+        first = pl.multiple_of((xs * lines_z + 2 * pair) * 2 * tok, rows_chunk)
+        rows = pl.ds(first, rows_chunk)
+
+        @pl.loop(0, half_units // cols_tile)
+        def _(tile):
+            at = pl.ds(pl.multiple_of(tile * cols_tile, cols_tile), cols_tile)
+            block = g[batch, rows, pl.ds(0, width)]
+            gate_act = jnp.dot(block, gate_w[:, at], preferred_element_type=jnp.float32)
+            up_act = jnp.dot(block, up_w[:, at], preferred_element_type=jnp.float32)
+            hidden[:, at] = (jax.nn.silu(gate_act) * up_act).astype(jnp.bfloat16)
+
+        lane = lax.broadcasted_iota(jnp.int32, (rows_chunk, 128), 1)
+        weights = g[batch, rows, pl.ds(width, 128)].astype(jnp.float32)
+        chosen = jnp.logical_or(lane == expert, lane == expert + 64)
+        scale = jnp.sum(jnp.where(chosen, weights, 0.0), axis=1, keepdims=True)
+
+        @pl.loop(0, width // cols_tile)
+        def _(tile):
+            at = pl.ds(pl.multiple_of(tile * cols_tile, cols_tile), cols_tile)
+            partial = jnp.dot(hidden[...], down_w[:, at], preferred_element_type=jnp.float32)
+            p[batch, rows, at] = (partial * scale).astype(jnp.bfloat16)
+
+        for zs in (2 * pair, 2 * pair + 1):
+            core_copy(batch, xs, zs).start()
+
+    def core_copy(batch, xs, zs):
+        index = xs * lines_z + zs
+        return pltpu.make_async_remote_copy(
+            src_ref=p.at[batch, at_rows(slot(xs, zs, other_core))],
+            dst_ref=core_in.at[batch, at_rows(index)],
+            send_sem=c_send.at[batch, index], recv_sem=c_recv.at[batch, index],
+            device_id=to_core, device_id_type=MESH,
+        )
+
+    def x_copy(batch, zs):
+        return pltpu.make_async_remote_copy(
+            src_ref=p.at[batch, at_rows(slot(other_x, zs, core))],
+            dst_ref=x_in.at[batch, at_rows(zs)],
+            send_sem=x_send.at[batch, zs], recv_sem=x_recv.at[batch, zs],
+            device_id=to_x, device_id_type=MESH,
+        )
+
+    def z_copy(batch, zs, place, target):
+        return pltpu.make_async_remote_copy(
+            src_ref=p.at[batch, at_rows(slot(x, zs, core))],
+            dst_ref=z_in.at[batch, at_rows(place)],
+            send_sem=z_send.at[batch, zs], recv_sem=z_recv.at[batch, place],
+            device_id=target, device_id_type=MESH,
+        )
+
+    def add(batch, index, source, place):
+        @pl.loop(0, tok // 16)
+        def _(part):
+            to = pl.ds(pl.multiple_of(index * tok + part * 16, 16), 16)
+            of = pl.ds(pl.multiple_of(place * tok + part * 16, 16), 16)
+            total = p[batch, to, :].astype(jnp.float32) + source[batch, of, :].astype(jnp.float32)
+            p[batch, to, :] = total.astype(jnp.bfloat16)
+
+    def core_add(batch, xs, zs):
+        core_copy(batch, xs, zs).wait_recv()
+        add(batch, slot(xs, zs, core), core_in, xs * lines_z + zs)
+
+    def in_order(body):
+        for zs, way in z_steps:
+            @pl.when(z < zs if way > 0 else z > zs)
+            def _():
+                body(zs, way)
+
+    def send_x(batch):
+        def one(zs, way):
+            core_add(batch, other_x, zs)
+            x_copy(batch, zs).start()
+
+        in_order(one)
+        one(z, 0)
+
+    def keep_x(batch):
+        @pl.loop(0, lines_z)
+        def _(zs):
+            core_add(batch, x, zs)
+
+    def sum_z(batch):
+        def one(zs, way):
+            x_copy(batch, zs).wait_recv()
+            index = slot(x, zs, core)
+            add(batch, index, x_in, zs)
+            if way > 0:
+                @pl.when(z > 0)
+                def _():
+                    z_copy(batch, zs, zs, to_high).wait_recv()
+                    add(batch, index, z_in, zs)
+
+                z_copy(batch, zs, zs, to_high).start()
+            else:
+                @pl.when(z < lines_z - 1)
+                def _():
+                    z_copy(batch, zs, zs, to_low).wait_recv()
+                    add(batch, index, z_in, zs)
+
+                place = jnp.where(z == zs + 1, lines_z, zs)
+                z_copy(batch, zs, place, to_low).start()
+
+        in_order(one)
+        x_copy(batch, z).wait_recv()
+        add(batch, mine, x_in, z)
+
+        @pl.when(z > 0)
+        def _():
+            z_copy(batch, z, z, to_high).wait_recv()
+            add(batch, mine, z_in, z)
+
+        @pl.when(z < lines_z - 1)
+        def _():
+            z_copy(batch, z, lines_z, to_low).wait_recv()
+            add(batch, mine, z_in, lines_z)
+
+        out[batch] = p[batch, at_rows(mine), :]
+
+    def reduce_sent(batch):
+        @pl.loop(0, lines_z)
+        def _(zs):
+            core_copy(batch, 0, zs).wait_send()
+            core_copy(batch, 1, zs).wait_send()
+            x_copy(batch, zs).wait_send()
+
+            @pl.when(zs != z)
+            def _():
+                z_copy(batch, zs, zs, to_x).wait_send()
+
+    gather_own(0)
+    for step in range(1, lines_z):
+        gather_forward(0, step)
+    gather_own(1)
+    gather_across(0)
+    gather_core(0)
+    for load in loads[2:]:
+        load.wait()
+    compute(0, other_x, 0)
+    gather_forward(1, 1)
+    compute(0, other_x, 1)
+    gather_forward(1, 2)
+    gather_forward(1, 3)
+    send_x(0)
+    compute(0, x, 0)
+    compute(0, x, 1)
+    keep_x(0)
+    gather_across(1)
+    gather_core(1)
+    compute(1, other_x, 0)
+    compute(1, other_x, 1)
+    send_x(1)
+    compute(1, x, 0)
+    compute(1, x, 1)
+    keep_x(1)
+    sum_z(0)
+    sum_z(1)
+    for batch in range(batches):
+        gather_sent(batch)
+        reduce_sent(batch)
+
+
+def gather_shards(tokens_in, expert_ids, gate_fixed, w_gate, w_up, w_down):
+    batches, tok, width = tokens_in.shape
+    half_units = w_gate.shape[2]
+    fixed_gate = gate_fixed.astype(jnp.float32)
+    weight = route_scale * fixed_gate / jnp.sum(fixed_gate, axis=2, keepdims=True)
+    named = expert_ids[:, :, :, None] == jnp.arange(64, dtype=jnp.int32)
+    dense = jnp.sum(jnp.where(named, weight[:, :, :, None], 0.0), axis=2)
+    high = dense.astype(jnp.bfloat16)
+    low = (dense - high.astype(jnp.float32)).astype(jnp.bfloat16)
+    cols = jnp.concatenate([high, low], axis=2)
+    total = 16 * tok
+    bf16 = jnp.bfloat16
+    dma = pltpu.SemaphoreType.DMA
+    anywhere = pl.BlockSpec(memory_space=pl.ANY)
+    vmem = pl.BlockSpec(memory_space=pltpu.VMEM)
+    return pl.pallas_call(
+        gather_kernel,
+        out_shape=jax.ShapeDtypeStruct((batches, tok, width), bf16),
+        in_specs=[anywhere, vmem, anywhere, anywhere, anywhere],
+        out_specs=vmem,
+        scratch_shapes=[
+            pltpu.VMEM((batches, total, width + 128), bf16),
+            pltpu.VMEM((batches, total, width), bf16),
+            pltpu.VMEM((batches, 8 * tok, width), bf16),
+            pltpu.VMEM((batches, 4 * tok, width), bf16),
+            pltpu.VMEM((batches, 5 * tok, width), bf16),
+            pltpu.VMEM((width, half_units), bf16),
+            pltpu.VMEM((width, half_units), bf16),
+            pltpu.VMEM((half_units, width), bf16),
+            pltpu.VMEM((rows_chunk, half_units), bf16),
+            dma((5,)),
+            dma((batches, 4, 16)),
+            dma((batches, 16)),
+            dma((batches, 8)),
+            dma((batches, 8)),
+            dma((batches, 4)),
+            dma((batches, 4)),
+            dma((batches, 4)),
+            dma((batches, 5)),
+        ],
+        compiler_params=pltpu.CompilerParams(
+            collective_id=0, has_side_effects=True, vmem_limit_bytes=63 * 1024 * 1024
+        ),
+        cost_estimate=pl.CostEstimate(
+            flops=6 * batches * total * width * half_units,
+            bytes_accessed=3 * 2 * width * half_units,
+            transcendentals=batches * total * half_units,
+        ),
+    )(tokens_in, cols, w_gate, w_up, w_down)
+
+
 def solution(mesh):
+    small = mesh.shape["node"] == 4 and mesh.shape["local"] == lines_z
     return jax.shard_map(
-        shards,
+        gather_shards if small else shards,
         mesh=mesh,
         in_specs=(
             P(None, ("groups", "node", "local"), None),

time: 462 us -> 217 us (0.47)
  waiting for transfers between devices: 365 us -> 0 us
  Pallas kernels: 0 us -> 212 us
  matrix products: 34.3 us -> 0 us
  starting transfers between devices: 21.5 us -> 0 us
  local copies, waits for them, and re-layouts: 22.5 us -> 2.16 us
  other arithmetic: 18.2 us -> 2.38 us
    all_to_all x4 -> x0, waiting for transfers between devices: 365 us -> none  [the longest x2 187 us: shards(): lax.all_to_all(copies, ('node', 'local'), split_axis=0, concat_axis=0, ti...]
    pallas_call x0 -> x1, Pallas kernels: none -> 212 us  [gather_shards(): pl.pallas_call(gather_kernel, out_shape=jax.ShapeDtypeStruct((batches, to...]
    dot_general x8 -> x0, matrix products: 34.3 us -> none  [the longest x2 12.2 us: expert_part(): jnp.dot(expert_rows, gate_half, preferred_element_type=jnp.float32)]
    all_to_all x4 -> x0, starting transfers between devices: 21.5 us -> none  [the longest x2 12.1 us: shards(): lax.all_to_all(copies, ('node', 'local'), split_axis=0, concat_axis=0, ti...]
    convert_element_type x2 -> x0, local copies, waits for them, and re-layouts: 9.04 us -> none  [shards(): lookup[position.reshape(-1)].reshape(tok_rows, top_count, width)]
    convert_element_type x6 -> x1, other arithmetic: 8.17 us -> 0.01 us  [gather_shards(): low = (dense - high.astype(jnp.float32)).astype(jnp.bfloat16)]
    reduce_sum x5 -> x1, other arithmetic: 7.47 us -> 0.89 us  [gather_shards(): dense = jnp.sum(jnp.where(named, weight[:, :, :, None], 0.0), axis=2)]
    gather x2 -> x0, local copies, waits for them, and re-layouts: 5.96 us -> none  [shards(): lookup[position.reshape(-1)].reshape(tok_rows, top_count, width)]
  transfers between devices with their start and end apart: 4 -> 0, of which waited for: 4 -> 0; matrix products, arithmetic and copies ran while one was open for 10% -> 0% of each run, Pallas kernels for 0% -> 0%
where the time goes in v1:
time: 217 us
  Pallas kernels  212 us (98%)
  other arithmetic  2.38 us (1%)
    pallas_call x1, Pallas kernels, gather_shards(): pl.pallas_call(gather_kernel, out_shape=jax.ShapeDtypeStruct((batches, to...  212 us

profile of v1, /device:TPU:0, one launch (start us, length us, event | category | flops | bytes accessed | tf_op | source)
XLA Modules:
  0.0 217.0 jit_solution(4039760652291517325)
XLA Ops:
  0.0 0.8 multiply_divide_fusion
  0.8 0.9 select_reduce_fusion
  1.7 0.7 pad_maximum_fusion.cols
  2.4 212.4 %shard_map.64 = bf16[2,64,3584]{2,1,0:T(8,128)(2,1)} custom-call(bf16[2,64,3584]{2,1,0:T(8,128)(2,1)} %tokens.1, bf16[2,64,128]{2,1,0:T(8,128)(2,1)} %pad_maximum_fusion.cols, bf16[1,3584,512]{2,1,0:T(8,128)(2,1)} %gate_hbm.1, bf16[1,3584,512]{2,1,0:T(8,128)(2,1)} %up_hbm.1, bf16[1,512,3584]{2,1,0:T(8,128)(2,1)} %down_hbm.1), custom_call_target="tpu_custom_call" | custom-call | flops 22548578304 | bytes 11010048 | tf_op jit(solution)/shard_map/pallas_call | solution.py:411
  214.8 2.2 copy.10
  (1 shorter events, 0.0 us)

commit v2 on v1

--- a/solution.py
+++ b/solution.py
@@ -9,8 +9,10 @@
 
 MESH = pl.DeviceIdType.MESH
 lines_z = 4
-rows_chunk = 256
-cols_tile = 256
+rows_chunk = 512
+cols_tile = 512
+side_cols = 256
+side_gather = 384
 
 route_scale = 2.5
 
@@ -91,8 +93,8 @@
 
 def gather_kernel(
     tokens, cols, gate_hbm, up_hbm, down_hbm, out,
-    g, p, core_in, x_in, z_in, gate_w, up_w, down_w, hidden,
-    load_sem, g_send, g_recv, c_send, c_recv, x_send, x_recv, z_send, z_recv,
+    g, p, core_in, x_in, z_in, b_in, gate_w, up_w, down_w, hidden,
+    load_sem, g_send, g_recv, gb_recv, c_send, c_recv, x_send, x_recv, z_send, z_recv, b_send, b_recv,
 ):
     batches, tok, width = tokens.shape
     half_units = gate_w.shape[1]
@@ -102,6 +104,10 @@
     x, core = node // 2, node % 2
     expert = node * (lines_z // 2) + z // 2
     other_x, other_core = 1 - x, 1 - core
+    g_main = pl.ds(0, width + 128 - side_gather)
+    g_side = pl.ds(width + 128 - side_gather, side_gather)
+    p_main, p_side = pl.ds(0, width - side_cols), pl.ds(width - side_cols, side_cols)
+    everything = pl.ds(0, width)
     to_x = (group, other_x * 2 + core, z)
     to_core = (group, x * 2 + other_core, z)
     to_high = (group, node, z + 1)
@@ -143,29 +149,42 @@
 
     pl.semaphore_wait(barrier, 3 + (z + 1) % lines_z // 2)
 
+    def remote(part, to, send, recv, target):
+        return pltpu.make_async_remote_copy(
+            src_ref=part, dst_ref=to, send_sem=send, recv_sem=recv,
+            device_id=target, device_id_type=MESH,
+        )
+
     def g_copy(batch, index, kind, target):
         part = g.at[batch, at_rows(index)]
-        return pltpu.make_async_remote_copy(
-            src_ref=part, dst_ref=part,
-            send_sem=g_send.at[batch, kind, index], recv_sem=g_recv.at[batch, index],
-            device_id=target, device_id_type=MESH,
-        )
+        return remote(part, part, g_send.at[batch, kind, index], g_recv.at[batch, index], target)
+
+    def g_copy_main(batch, index):
+        part = g.at[batch, at_rows(index), g_main]
+        return remote(part, part, g_send.at[batch, 2, index], g_recv.at[batch, index], to_x)
+
+    def g_copy_side(batch, index, kind, target):
+        part = g.at[batch, at_rows(index), g_side]
+        return remote(part, part, g_send.at[batch, kind, index], gb_recv.at[batch, index], target)
 
     def arrived(batch, index):
         g_copy(batch, index, 3, to_core).wait_recv()
 
-    def gather_own(batch):
+    def both_ways(copy, batch, index):
+        @pl.when(z < lines_z - 1)
+        def _():
+            copy(batch, index, 0, to_high).start()
+
+        @pl.when(z > 0)
+        def _():
+            copy(batch, index, 1, to_low).start()
+
+    def gather_own_x(batch):
         loads[batch].wait()
         g_copy(batch, mine, 2, to_x).start()
 
-        @pl.when(z < lines_z - 1)
-        def _():
-            g_copy(batch, mine, 0, to_high).start()
-
-        @pl.when(z > 0)
-        def _():
-            g_copy(batch, mine, 1, to_low).start()
-
+    def gather_own(batch):
+        both_ways(g_copy, batch, mine)
         g_copy(batch, mine, 3, to_core).start()
 
     def gather_forward(batch, step):
@@ -178,7 +197,7 @@
             def _():
                 g_copy(batch, index, 0, to_high).start()
 
-            g_copy(batch, index, 2, to_x).start()
+            g_copy_main(batch, index).start()
             g_copy(batch, index, 3, to_core).start()
 
         @pl.when(z + step < lines_z)
@@ -190,50 +209,85 @@
             def _():
                 g_copy(batch, index, 1, to_low).start()
 
-            g_copy(batch, index, 2, to_x).start()
+            g_copy_main(batch, index).start()
             g_copy(batch, index, 3, to_core).start()
 
-    def gather_across(batch):
+    def forward_side(batch, step):
+        @pl.when(z >= step)
+        def _():
+            index = slot(other_x, z - step, core)
+            g_copy_side(batch, index, 0, to_x).wait_recv()
+
+            @pl.when(z < lines_z - 1)
+            def _():
+                g_copy_side(batch, index, 0, to_high).start()
+
+        @pl.when(z + step < lines_z)
+        def _():
+            index = slot(other_x, z + step, core)
+            g_copy_side(batch, index, 0, to_x).wait_recv()
+
+            @pl.when(z > 0)
+            def _():
+                g_copy_side(batch, index, 1, to_low).start()
+
+    def across_own(batch):
+        index = slot(other_x, z, core)
+        arrived(batch, index)
+        both_ways(g_copy_side, batch, index)
+        g_copy(batch, index, 3, to_core).start()
+
+    def gather_across(batch, step):
         def one(zs):
             index = slot(other_x, zs, core)
-            arrived(batch, index)
+            g_copy_main(batch, index).wait_recv()
             g_copy(batch, index, 3, to_core).start()
 
-        one(z)
-        for step in range(1, lines_z):
-            @pl.when(z >= step)
-            def _():
-                one(z - step)
-
-            @pl.when(z + step < lines_z)
-            def _():
-                one(z + step)
-
-    def gather_core(batch):
-        @pl.loop(0, 2 * lines_z)
-        def _(index):
-            arrived(batch, index * 2 + other_core)
+        @pl.when(z >= step)
+        def _():
+            one(z - step)
+
+        @pl.when(z + step < lines_z)
+        def _():
+            one(z + step)
+
+    def gather_core(batch, xs):
+        @pl.loop(0, lines_z)
+        def _(zs):
+            arrived(batch, slot(xs, zs, other_core))
 
     def gather_sent(batch):
         @pl.loop(0, lines_z)
         def _(zs):
             index = slot(x, zs, core)
+            across = slot(other_x, zs, core)
 
             @pl.when(jnp.logical_and(z < lines_z - 1, zs <= z))
             def _():
                 g_copy(batch, index, 0, to_high).wait_send()
+                g_copy_side(batch, across, 0, to_high).wait_send()
 
             @pl.when(jnp.logical_and(z > 0, zs >= z))
             def _():
                 g_copy(batch, index, 1, to_low).wait_send()
-
-            g_copy(batch, index, 2, to_x).wait_send()
+                g_copy_side(batch, across, 1, to_low).wait_send()
+
+            @pl.when(zs == z)
+            def _():
+                g_copy(batch, index, 2, to_x).wait_send()
+
+            @pl.when(zs != z)
+            def _():
+                g_copy_main(batch, index).wait_send()
+
             g_copy(batch, index, 3, to_core).wait_send()
-            g_copy(batch, slot(other_x, zs, core), 3, to_core).wait_send()
-
-    def compute(batch, xs, pair):
-        first = pl.multiple_of((xs * lines_z + 2 * pair) * 2 * tok, rows_chunk)
-        rows = pl.ds(first, rows_chunk)
+            g_copy(batch, across, 3, to_core).wait_send()
+
+    def chunk(xs):
+        return pl.ds(pl.multiple_of(xs * rows_chunk, rows_chunk), rows_chunk)
+
+    def compute_hidden(batch, xs):
+        rows = chunk(xs)
 
         @pl.loop(0, half_units // cols_tile)
         def _(tile):
@@ -243,6 +297,8 @@
             up_act = jnp.dot(block, up_w[:, at], preferred_element_type=jnp.float32)
             hidden[:, at] = (jax.nn.silu(gate_act) * up_act).astype(jnp.bfloat16)
 
+    def compute_down(batch, xs):
+        rows = chunk(xs)
         lane = lax.broadcasted_iota(jnp.int32, (rows_chunk, 128), 1)
         weights = g[batch, rows, pl.ds(width, 128)].astype(jnp.float32)
         chosen = jnp.logical_or(lane == expert, lane == expert + 64)
@@ -254,7 +310,7 @@
             partial = jnp.dot(hidden[...], down_w[:, at], preferred_element_type=jnp.float32)
             p[batch, rows, at] = (partial * scale).astype(jnp.bfloat16)
 
-        for zs in (2 * pair, 2 * pair + 1):
+        for zs in range(lines_z):
             core_copy(batch, xs, zs).start()
 
     def core_copy(batch, xs, zs):
@@ -266,36 +322,37 @@
             device_id=to_core, device_id_type=MESH,
         )
 
-    def x_copy(batch, zs):
-        return pltpu.make_async_remote_copy(
-            src_ref=p.at[batch, at_rows(slot(other_x, zs, core))],
-            dst_ref=x_in.at[batch, at_rows(zs)],
-            send_sem=x_send.at[batch, zs], recv_sem=x_recv.at[batch, zs],
-            device_id=to_x, device_id_type=MESH,
+    def x_copy(batch, zs, span):
+        return remote(
+            p.at[batch, at_rows(slot(other_x, zs, core)), span], x_in.at[batch, at_rows(zs), span],
+            x_send.at[batch, zs], x_recv.at[batch, zs], to_x,
         )
 
     def z_copy(batch, zs, place, target):
-        return pltpu.make_async_remote_copy(
-            src_ref=p.at[batch, at_rows(slot(x, zs, core))],
-            dst_ref=z_in.at[batch, at_rows(place)],
-            send_sem=z_send.at[batch, zs], recv_sem=z_recv.at[batch, place],
-            device_id=target, device_id_type=MESH,
-        )
-
-    def add(batch, index, source, place):
+        return remote(
+            p.at[batch, at_rows(slot(x, zs, core))], z_in.at[batch, at_rows(place)],
+            z_send.at[batch, zs], z_recv.at[batch, place], target,
+        )
+
+    def side_copy(batch, zs, place, target):
+        return remote(
+            p.at[batch, at_rows(slot(other_x, zs, core)), p_side], b_in.at[batch, at_rows(place)],
+            b_send.at[batch, zs], b_recv.at[batch, place], target,
+        )
+
+    def add(batch, index, span, source, place, source_span):
         @pl.loop(0, tok // 16)
         def _(part):
             to = pl.ds(pl.multiple_of(index * tok + part * 16, 16), 16)
             of = pl.ds(pl.multiple_of(place * tok + part * 16, 16), 16)
-            total = p[batch, to, :].astype(jnp.float32) + source[batch, of, :].astype(jnp.float32)
-            p[batch, to, :] = total.astype(jnp.bfloat16)
+            p[batch, to, span] = p[batch, to, span] + source[batch, of, source_span]
 
     def core_add(batch, xs, zs):
         core_copy(batch, xs, zs).wait_recv()
-        add(batch, slot(xs, zs, core), core_in, xs * lines_z + zs)
-
-    def in_order(body):
-        for zs, way in z_steps:
+        add(batch, slot(xs, zs, core), everything, core_in, xs * lines_z + zs, everything)
+
+    def in_order(body, steps=(0, 1, 2)):
+        for zs, way in [z_steps[2 * step + side] for step in steps for side in range(2)]:
             @pl.when(z < zs if way > 0 else z > zs)
             def _():
                 body(zs, way)
@@ -303,51 +360,70 @@
     def send_x(batch):
         def one(zs, way):
             core_add(batch, other_x, zs)
-            x_copy(batch, zs).start()
+            x_copy(batch, zs, p_main).start()
 
         in_order(one)
-        one(z, 0)
+        core_add(batch, other_x, z)
 
     def keep_x(batch):
         @pl.loop(0, lines_z)
         def _(zs):
             core_add(batch, x, zs)
 
-    def sum_z(batch):
+    def line_step(batch, zs, way, copy, index, span, source, source_span):
+        if way > 0:
+            @pl.when(z > 0)
+            def _():
+                copy(batch, zs, zs, to_high).wait_recv()
+                add(batch, index, span, source, zs, source_span)
+
+            copy(batch, zs, zs, to_high).start()
+        else:
+            @pl.when(z < lines_z - 1)
+            def _():
+                copy(batch, zs, zs, to_low).wait_recv()
+                add(batch, index, span, source, zs, source_span)
+
+            place = jnp.where(z == zs + 1, lines_z, zs)
+            copy(batch, zs, place, to_low).start()
+
+    def line_end(batch, copy, index, span, source, source_span):
+        @pl.when(z > 0)
+        def _():
+            copy(batch, z, z, to_high).wait_recv()
+            add(batch, index, span, source, z, source_span)
+
+        @pl.when(z < lines_z - 1)
+        def _():
+            copy(batch, z, lines_z, to_low).wait_recv()
+            add(batch, index, span, source, lines_z, source_span)
+
+    def sum_side(batch, steps):
+        whole_side = pl.ds(0, side_cols)
+
         def one(zs, way):
-            x_copy(batch, zs).wait_recv()
+            index = slot(other_x, zs, core)
+            line_step(batch, zs, way, side_copy, index, p_side, b_in, whole_side)
+
+        in_order(one, steps)
+
+    def side_end(batch):
+        line_end(batch, side_copy, slot(other_x, z, core), p_side, b_in, pl.ds(0, side_cols))
+        x_copy(batch, z, everything).start()
+
+    def sum_z(batch, steps):
+        def one(zs, way):
+            x_copy(batch, zs, p_main).wait_recv()
             index = slot(x, zs, core)
-            add(batch, index, x_in, zs)
-            if way > 0:
-                @pl.when(z > 0)
-                def _():
-                    z_copy(batch, zs, zs, to_high).wait_recv()
-                    add(batch, index, z_in, zs)
-
-                z_copy(batch, zs, zs, to_high).start()
-            else:
-                @pl.when(z < lines_z - 1)
-                def _():
-                    z_copy(batch, zs, zs, to_low).wait_recv()
-                    add(batch, index, z_in, zs)
-
-                place = jnp.where(z == zs + 1, lines_z, zs)
-                z_copy(batch, zs, place, to_low).start()
-
-        in_order(one)
-        x_copy(batch, z).wait_recv()
-        add(batch, mine, x_in, z)
-
-        @pl.when(z > 0)
-        def _():
-            z_copy(batch, z, z, to_high).wait_recv()
-            add(batch, mine, z_in, z)
-
-        @pl.when(z < lines_z - 1)
-        def _():
-            z_copy(batch, z, lines_z, to_low).wait_recv()
-            add(batch, mine, z_in, lines_z)
-
+            add(batch, index, p_main, x_in, zs, p_main)
+            line_step(batch, zs, way, z_copy, index, everything, z_in, everything)
+
+        in_order(one, steps)
+
+    def sum_end(batch):
+        x_copy(batch, z, everything).wait_recv()
+        add(batch, mine, everything, x_in, z, everything)
+        line_end(batch, z_copy, mine, everything, z_in, everything)
         out[batch] = p[batch, at_rows(mine), :]
 
     def reduce_sent(batch):
@@ -355,39 +431,73 @@
         def _(zs):
             core_copy(batch, 0, zs).wait_send()
             core_copy(batch, 1, zs).wait_send()
-            x_copy(batch, zs).wait_send()
+
+            @pl.when(zs == z)
+            def _():
+                x_copy(batch, zs, everything).wait_send()
 
             @pl.when(zs != z)
             def _():
+                x_copy(batch, zs, p_main).wait_send()
                 z_copy(batch, zs, zs, to_x).wait_send()
-
+                side_copy(batch, zs, zs, to_x).wait_send()
+
+    gather_own_x(0)
     gather_own(0)
-    for step in range(1, lines_z):
-        gather_forward(0, step)
+    across_own(0)
+    gather_forward(0, 1)
+    gather_own_x(1)
+    forward_side(0, 1)
+    gather_forward(0, 2)
+    forward_side(0, 2)
     gather_own(1)
-    gather_across(0)
-    gather_core(0)
+    gather_forward(0, 3)
+    forward_side(0, 3)
+    gather_core(0, x)
     for load in loads[2:]:
         load.wait()
-    compute(0, other_x, 0)
+    compute_hidden(0, x)
+    gather_across(0, 1)
+    across_own(1)
+    compute_down(0, x)
     gather_forward(1, 1)
-    compute(0, other_x, 1)
+    gather_across(0, 2)
+    forward_side(1, 1)
+    gather_across(0, 3)
     gather_forward(1, 2)
+    forward_side(1, 2)
+    gather_core(0, other_x)
+    compute_hidden(0, other_x)
     gather_forward(1, 3)
+    forward_side(1, 3)
+    compute_down(0, other_x)
     send_x(0)
-    compute(0, x, 0)
-    compute(0, x, 1)
     keep_x(0)
-    gather_across(1)
-    gather_core(1)
-    compute(1, other_x, 0)
-    compute(1, other_x, 1)
+    sum_side(0, (0,))
+    gather_core(1, x)
+    gather_across(1, 1)
+    compute_hidden(1, x)
+    sum_side(0, (1,))
+    gather_across(1, 2)
+    compute_down(1, x)
+    sum_side(0, (2,))
+    gather_across(1, 3)
+    side_end(0)
+    gather_core(1, other_x)
+    compute_hidden(1, other_x)
+    compute_down(1, other_x)
+    sum_z(0, (0,))
     send_x(1)
-    compute(1, x, 0)
-    compute(1, x, 1)
+    sum_side(1, (0,))
+    sum_z(0, (1,))
+    sum_side(1, (1,))
     keep_x(1)
-    sum_z(0)
-    sum_z(1)
+    sum_z(0, (2,))
+    sum_side(1, (2,))
+    side_end(1)
+    sum_end(0)
+    sum_z(1, (0, 1, 2))
+    sum_end(1)
     for batch in range(batches):
         gather_sent(batch)
         reduce_sent(batch)
@@ -419,6 +529,7 @@
             pltpu.VMEM((batches, 8 * tok, width), bf16),
             pltpu.VMEM((batches, 4 * tok, width), bf16),
             pltpu.VMEM((batches, 5 * tok, width), bf16),
+            pltpu.VMEM((batches, 5 * tok, side_cols), bf16),
             pltpu.VMEM((width, half_units), bf16),
             pltpu.VMEM((width, half_units), bf16),
             pltpu.VMEM((half_units, width), bf16),
@@ -426,10 +537,13 @@
             dma((5,)),
             dma((batches, 4, 16)),
             dma((batches, 16)),
+            dma((batches, 16)),
             dma((batches, 8)),
             dma((batches, 8)),
             dma((batches, 4)),
             dma((batches, 4)),
+            dma((batches, 4)),
+            dma((batches, 5)),
             dma((batches, 4)),
             dma((batches, 5)),
         ],

time: 217 us -> 184 us (0.85)
  Pallas kernels: 212 us -> 179 us
    pallas_call x1, Pallas kernels: 212 us -> 179 us  [gather_shards(): pl.pallas_call(gather_kernel, out_shape=jax.ShapeDtypeStruct((batches, to...]
where the time goes in v2:
time: 184 us
  Pallas kernels  179 us (97%)
  other arithmetic  2.38 us (1%)
  local copies, waits for them, and re-layouts  2.16 us (1%)
    pallas_call x1, Pallas kernels, gather_shards(): pl.pallas_call(gather_kernel, out_shape=jax.ShapeDtypeStruct((batches, to...  179 us

profile of v2, /device:TPU:0, one launch (start us, length us, event | category | flops | bytes accessed | tf_op | source)
XLA Modules:
  0.0 184.0 jit_solution(16658531167164290474)
XLA Ops:
  0.0 0.8 multiply_divide_fusion
  0.8 0.9 select_reduce_fusion
  1.7 0.7 pad_maximum_fusion.cols
  2.4 179.5 %shard_map.64 = bf16[2,64,3584]{2,1,0:T(8,128)(2,1)} custom-call(bf16[2,64,3584]{2,1,0:T(8,128)(2,1)} %tokens.1, bf16[2,64,128]{2,1,0:T(8,128)(2,1)} %pad_maximum_fusion.cols, bf16[1,3584,512]{2,1,0:T(8,128)(2,1)} %gate_hbm.1, bf16[1,3584,512]{2,1,0:T(8,128)(2,1)} %up_hbm.1, bf16[1,512,3584]{2,1,0:T(8,128)(2,1)} %down_hbm.1), custom_call_target="tpu_custom_call" | custom-call | flops 22548578304 | bytes 11010048 | tf_op jit(solution)/shard_map/pallas_call | solution.py:521
  181.9 2.2 %copy.10 = bf16[2,64,3584]{2,1,0:T(8,128)(2,1)} copy(bf16[2,64,3584]{2,1,0:T(8,128)(2,1)} %shard_map.64) | data formatting | bytes 1835008
  (1 shorter events, 0.0 us)

commit v3 on v2

--- a/solution.py
+++ b/solution.py
@@ -88,11 +88,15 @@
     return jnp.stack(results)
 
 
-z_steps = ((3, 1), (0, -1), (2, 1), (1, -1), (1, 1), (2, -1))
+z_steps = (
+    ((3, 1, 0, 1), (0, -1, 2, 3)),
+    ((2, 1, 0, 1), (1, -1, 2, 3)),
+    ((1, 1, 0, 0), (2, -1, 3, 3), (0, -1, 1, 1), (3, 1, 2, 2)),
+)
 
 
 def gather_kernel(
-    tokens, cols, gate_hbm, up_hbm, down_hbm, out,
+    tokens, ids, gates, gate_hbm, up_hbm, down_hbm, out,
     g, p, core_in, x_in, z_in, b_in, gate_w, up_w, down_w, hidden,
     load_sem, g_send, g_recv, gb_recv, c_send, c_recv, x_send, x_recv, z_send, z_recv, b_send, b_recv,
 ):
@@ -133,7 +137,16 @@
     for load in loads:
         load.start()
     for batch in range(batches):
-        g[batch, at_rows(mine), pl.ds(width, 128)] = cols[batch]
+        fixed_gate = gates[batch].astype(jnp.float32)
+        weight = route_scale * fixed_gate / jnp.sum(fixed_gate, axis=1, keepdims=True)
+        lane = lax.broadcasted_iota(jnp.int32, (tok, 128), 1)
+        dense = jnp.zeros((tok, 128), jnp.float32)
+        for k in range(ids.shape[2]):
+            named = ids[batch, :, k : k + 1] == lane % 64
+            dense += jnp.where(named, weight[:, k : k + 1], 0.0)
+        high = dense.astype(jnp.bfloat16).astype(jnp.float32)
+        cols = jnp.where(lane < 64, high, dense - high).astype(jnp.bfloat16)
+        g[batch, at_rows(mine), pl.ds(width, 128)] = cols
 
     barrier = pltpu.get_barrier_semaphore()
     pl.semaphore_signal(barrier, inc=1, device_id=to_x, device_id_type=MESH)
@@ -352,8 +365,8 @@
         add(batch, slot(xs, zs, core), everything, core_in, xs * lines_z + zs, everything)
 
     def in_order(body, steps=(0, 1, 2)):
-        for zs, way in [z_steps[2 * step + side] for step in steps for side in range(2)]:
-            @pl.when(z < zs if way > 0 else z > zs)
+        for zs, way, first, last in [entry for step in steps for entry in z_steps[step]]:
+            @pl.when(jnp.logical_and(z >= first, z <= last))
             def _():
                 body(zs, way)
 
@@ -486,8 +499,8 @@
     gather_core(1, other_x)
     compute_hidden(1, other_x)
     compute_down(1, other_x)
+    send_x(1)
     sum_z(0, (0,))
-    send_x(1)
     sum_side(1, (0,))
     sum_z(0, (1,))
     sum_side(1, (1,))
@@ -506,13 +519,6 @@
 def gather_shards(tokens_in, expert_ids, gate_fixed, w_gate, w_up, w_down):
     batches, tok, width = tokens_in.shape
     half_units = w_gate.shape[2]
-    fixed_gate = gate_fixed.astype(jnp.float32)
-    weight = route_scale * fixed_gate / jnp.sum(fixed_gate, axis=2, keepdims=True)
-    named = expert_ids[:, :, :, None] == jnp.arange(64, dtype=jnp.int32)
-    dense = jnp.sum(jnp.where(named, weight[:, :, :, None], 0.0), axis=2)
-    high = dense.astype(jnp.bfloat16)
-    low = (dense - high.astype(jnp.float32)).astype(jnp.bfloat16)
-    cols = jnp.concatenate([high, low], axis=2)
     total = 16 * tok
     bf16 = jnp.bfloat16
     dma = pltpu.SemaphoreType.DMA
@@ -521,7 +527,7 @@
     return pl.pallas_call(
         gather_kernel,
         out_shape=jax.ShapeDtypeStruct((batches, tok, width), bf16),
-        in_specs=[anywhere, vmem, anywhere, anywhere, anywhere],
+        in_specs=[anywhere, vmem, vmem, anywhere, anywhere, anywhere],
         out_specs=vmem,
         scratch_shapes=[
             pltpu.VMEM((batches, total, width + 128), bf16),
@@ -555,7 +561,7 @@
             bytes_accessed=3 * 2 * width * half_units,
             transcendentals=batches * total * half_units,
         ),
-    )(tokens_in, cols, w_gate, w_up, w_down)
+    )(tokens_in, expert_ids, gate_fixed, w_gate, w_up, w_down)
 
 
 def solution(mesh):

time: 184 us -> 179 us (0.973)
  Pallas kernels: 179 us -> 174 us
  local copies, waits for them, and re-layouts: 2.16 us -> 4.99 us
  other arithmetic: 2.38 us -> 0 us
    pallas_call x1, Pallas kernels: 179 us -> 174 us  [gather_shards(): pl.pallas_call(gather_kernel, out_shape=jax.ShapeDtypeStruct((batches, to...]
    unnamed x1 -> x3, local copies, waits for them, and re-layouts: 2.16 us -> 4.99 us
where the time goes in v3:
time: 179 us
  Pallas kernels  174 us (97%)
  local copies, waits for them, and re-layouts  4.99 us (3%)
    pallas_call x1, Pallas kernels, gather_shards(): pl.pallas_call(gather_kernel, out_shape=jax.ShapeDtypeStruct((batches, to...  174 us
    unnamed x3, local copies, waits for them, and re-layouts  4.99 us

profile of v3, /device:TPU:0, one launch (start us, length us, event | category | flops | bytes accessed | tf_op | source)
XLA Modules:
  0.0 179.1 jit_solution(13459836233768402918)
XLA Ops:
  0.0 1.4 copy.7.ids
  1.4 1.4 copy.8.gates
  2.8 174.1 %shard_map.64 = bf16[2,64,3584]{2,1,0:T(8,128)(2,1)} custom-call(bf16[2,64,3584]{2,1,0:T(8,128)(2,1)} %tokens.1, s32[2,64,4]{2,1,0:T(8,128)} %copy.7.ids, s32[2,64,4]{2,1,0:T(8,128)} %copy.8.gates, bf16[1,3584,512]{2,1,0:T(8,128)(2,1)} %gate_hbm.1, bf16[1,3584,512]{2,1,0:T(8,128)(2,1)} %up_hbm.1, bf16[1,512,3584]{2,1,0:T(8,128)(2,1)} %down_hbm.1), custom_call_target="tpu_custom_call" | custom-call | flops 22548578304 | bytes 11010048 | tf_op jit(solution)/shard_map/pallas_call | solution.py:527
  176.9 2.2 %copy.10 = bf16[2,64,3584]{2,1,0:T(8,128)(2,1)} copy(bf16[2,64,3584]{2,1,0:T(8,128)(2,1)} %shard_map.64) | data formatting | bytes 1835008

commit v4 on v3

--- a/solution.py
+++ b/solution.py
@@ -508,8 +508,9 @@
     sum_z(0, (2,))
     sum_side(1, (2,))
     side_end(1)
+    sum_z(1, (0,))
     sum_end(0)
-    sum_z(1, (0, 1, 2))
+    sum_z(1, (1, 2))
     sum_end(1)
     for batch in range(batches):
         gather_sent(batch)

time: 179 us -> 179 us (level)
  no operation moved by 1% of the time
where the time goes in v4:
time: 179 us
  Pallas kernels  174 us (97%)
  local copies, waits for them, and re-layouts  4.99 us (3%)
    pallas_call x1, Pallas kernels, gather_shards(): pl.pallas_call(gather_kernel, out_shape=jax.ShapeDtypeStruct((batches, to...  174 us
    unnamed x3, local copies, waits for them, and re-layouts  4.99 us

profile of v4, /device:TPU:0, one launch (start us, length us, event | category | flops | bytes accessed | tf_op | source)
XLA Modules:
  0.0 178.9 jit_solution(4328657963292966895)
XLA Ops:
  0.0 1.4 copy.7.ids
  1.4 1.4 copy.8.gates
  2.8 173.9 %shard_map.64 = bf16[2,64,3584]{2,1,0:T(8,128)(2,1)} custom-call(bf16[2,64,3584]{2,1,0:T(8,128)(2,1)} %tokens.1, s32[2,64,4]{2,1,0:T(8,128)} %copy.7.ids, s32[2,64,4]{2,1,0:T(8,128)} %copy.8.gates, bf16[1,3584,512]{2,1,0:T(8,128)(2,1)} %gate_hbm.1, bf16[1,3584,512]{2,1,0:T(8,128)(2,1)} %up_hbm.1, bf16[1,512,3584]{2,1,0:T(8,128)(2,1)} %down_hbm.1), custom_call_target="tpu_custom_call" | custom-call | flops 22548578304 | bytes 11010048 | tf_op jit(solution)/shard_map/pallas_call | solution.py:528
  176.7 2.2 %copy.10 = bf16[2,64,3584]{2,1,0:T(8,128)(2,1)} copy(bf16[2,64,3584]{2,1,0:T(8,128)(2,1)} %shard_map.64) | data formatting | bytes 1835008
